TPU v7x, 256 devices: a whole 4x4x8 slice. The times are simulated.
256 devices in a mesh: row: 64 (over x, z, y_hi), col: 4 (over y_lo, core).
Axes of the slice: x: 4, y: 4 (y_hi: 2, y_lo: 2; y = y_hi * 2 + y_lo), z: 8, core: 2. Of those that a mesh axis runs over, the one named last changes fastest.
Arguments:
- eigvecs: bfloat16 [196608, 3072], P('row', 'col'), may hold values from -6 to 6
- panels: bfloat16 [196608, 512], P('row', 'col'), may hold values from -1 to 1
- t_factors: float32 [2, 256, 256], replicated, may hold values from -1 to 1, as said below
Outputs:
- transformed: bfloat16 [196608, 3072], P('row', 'col')
Inputs may be any that keep to these rules, and one draw needn't show every extreme that they name: `t_factors`: each of the two factors is upper triangular with a positive diagonal.
All inputs are finite; a program needn't handle non-finite values.
Results may differ from a plain program's by a relative error of at most 0.0053.
Values may be sent and summed in bfloat16 or wider, within the bound.
A program may use at most 64 MiB of HBM per device.

v0:
```python
import jax
import jax.numpy as jnp
from jax import lax
from jax.sharding import PartitionSpec as P


def apply_factor(factor, columns):
    return jnp.dot(factor, columns, precision=lax.Precision.HIGHEST).astype(jnp.bfloat16)


def finish(partial_value, factor):
    summed = lax.psum(partial_value, "row")
    return apply_factor(factor, summed)


def per_device(eigvecs, panels, t_factors):
    width = t_factors.shape[1]
    gathered = lax.all_gather(panels, "col", axis=1, tiled=True)
    leading = gathered[:, :width]
    trailing = gathered[:, width:]
    projected = jnp.einsum("rp,rc->pc", gathered, eigvecs, preferred_element_type=jnp.float32)
    coupling = jnp.einsum("rp,rq->pq", trailing, leading, preferred_element_type=jnp.float32)
    y_lead = finish(projected[:width], t_factors[0])
    local_second = projected[width:] - jnp.dot(
        coupling, y_lead.astype(jnp.float32), precision=lax.Precision.HIGHEST
    )
    y_trail = finish(local_second, t_factors[1])
    stacked = jnp.concatenate([y_lead, y_trail], axis=0)
    update = jnp.dot(gathered, stacked, preferred_element_type=jnp.float32)
    return (eigvecs.astype(jnp.float32) - update).astype(jnp.bfloat16)


def solution(mesh):
    in_specs = (P("row", "col"), P("row", "col"), P())
    out_specs = P("row", "col")
    return jax.shard_map(
        per_device, mesh=mesh, in_specs=in_specs, out_specs=out_specs, check_vma=False
    )
```

profile of v0, /device:TPU:4, one launch (start us, length us, event | category | flops | bytes accessed | tf_op | source)
XLA Modules:
  0.0 1390.6 jit_solution(3643414550969370810)
XLA Ops:
  6.5 0.0 all-gather.2.cloned.1.call-start
  6.5 0.7 all-gather.2.cloned.1.call-update
  7.3 0.0 all-reduce.3.cloned.1.call-start
  7.3 43.9 %all-gather.2.cloned.1.call-done = bf16[3072,512]{1,0:T(8,128)(2,1)} async-done(((bf16[3072,128]{1,0:T(8,128)(2,1)}), bf16[3072,512]{1,0:T(8,128)(2,1)}) %all-gather.2.cloned.1.call-update) | async-done | bytes 3145744 | tf_op jit(solution)/shard_map/all_gather | solution.py:18
  51.2 5.9 fusion.13
  57.2 0.0 copy-start
  57.2 0.9 slice.24
  58.1 0.0 all-reduce.3.cloned.1.call-update
  58.1 0.0 all-reduce.5.cloned.1.call-start
  58.2 2.5 fusion.1
  60.7 642.4 %all-reduce.3.cloned.1.call-done = f32[256,768]{1,0:T(8,128)} async-done(((f32[256,768]{1,0:T(8,128)}), f32[256,768]{1,0:T(8,128)}) %all-reduce.3.cloned.1.call-update) | async-done | bytes 786448 | tf_op jit(solution)/shard_map/psum | solution.py:12
  703.1 0.0 copy-done
  703.1 2.0 convolution_convert_fusion.1
  705.1 1.4 convolution_subtract_fusion
  706.5 0.0 all-reduce.5.cloned.1.call-update
  706.5 6.6 copy.4
  713.2 655.3 %all-reduce.5.cloned.1.call-done = f32[256,768]{1,0:T(8,128)} async-done(((f32[256,768]{1,0:T(8,128)}), f32[256,768]{1,0:T(8,128)}) %all-reduce.5.cloned.1.call-update) | async-done | bytes 786448 | tf_op jit(solution)/shard_map/psum | solution.py:12
  1368.5 2.0 fusion.4
  1370.5 7.0 fusion
  1377.5 6.6 copy.5
Async XLA Ops:
  6.5 44.7 %all-gather.2.cloned.1.call-start = ((), (), s32[]{:S(2)}) async-start(), calls=%async_computation | async-start | bytes 3932160 | tf_op jit(solution)/shard_map/all_gather | solution.py:18
  7.3 695.9 %all-reduce.3.cloned.1.call-start = ((), (), s32[]{:S(2)}) async-start(), calls=%async_computation.1 | async-start | bytes 1572864 | tf_op jit(solution)/shard_map/psum | solution.py:12
  57.2 645.9 %copy-start = (f32[2,256,256]{2,1,0:T(8,128)S(1)}, f32[2,256,256]{2,1,0:T(8,128)}, u32[]{:S(2)}) copy-start(f32[2,256,256]{2,1,0:T(8,128)} %param.5) | copy-start | bytes 1572868
  58.1 1310.3 %all-reduce.5.cloned.1.call-start = ((), (), s32[]{:S(2)}) async-start(), calls=%async_computation.2 | async-start | bytes 1572864 | tf_op jit(solution)/shard_map/psum | solution.py:12
Sparse Core Ops, SparseCore 0:
  9.2 42.0 all-gather.1
  58.3 644.8 all-reduce.2
  706.7 661.7 all-reduce.4
where the time goes:
time: 1410 us; the launch traced here: 1390 us
  waiting for transfers between devices  1340 us (95%)
  matrix products  20.8 us (1%)
  local copies, waits for them, and re-layouts  14.2 us (1%)
    psum x2, waiting for transfers between devices, finish(): summed = lax.psum(partial_value, 'row')  1300 us
    all_gather x1, waiting for transfers between devices, per_device(): gathered = lax.all_gather(panels, 'col', axis=1, tiled=True)  43.9 us
  transfers between devices with their start and end apart: 3, of which 3 were waited for; matrix products, arithmetic and copies ran while one was open for 1% of the time, Pallas kernels for 0%

commit v1 on v0

v1 whole, which is shorter than its diff:
```python
import functools

import jax
import jax.numpy as jnp
from jax import lax
from jax.experimental import pallas as pl
from jax.experimental.pallas import tpu as pltpu
from jax.sharding import PartitionSpec as P

MESH = pl.DeviceIdType.MESH
NX, NZ = 4, 8
ROWS = 3072
COLS = 768
W = 128
WIDE = COLS + 2 * W
HALF = ROWS // 2
CHUNKS = 3
CHUNK = HALF // CHUNKS
GROUPS = (64, 32, 32)
BF16 = jnp.bfloat16
F32 = jnp.float32


def tdot(a, b):
    return lax.dot_general(a, b, (((0,), (0,)), ((), ())), preferred_element_type=F32)


def dot(a, b):
    return jnp.dot(a, b, preferred_element_type=F32)


def split(value):
    high = value.astype(BF16)
    return high, (value - high.astype(F32)).astype(BF16)


def place():
    row, col = lax.axis_index("row"), lax.axis_index("col")
    return row // 16, lax.rem(row // 2, 8), lax.rem(row, 2), col // 2, lax.rem(col, 2)


def device(x, z, y_hi, y_lo, core):
    return ((x * NZ + z) * 2 + y_hi, y_lo * 2 + core)


class Group:
    def __init__(self, depth, refs):
        self.depth = depth
        (self.acc, self.xs, self.xr, self.zf, self.zs, self.zr, self.yf, self.yr, self.full, self.sem3, self.sem7, self.sem1) = refs

    def bind(self, x, z, y_hi, y_lo, core):
        self.x, self.z = x, z
        self.x_peer = [device(lax.rem(x + d, NX), z, y_hi, y_lo, core) for d in range(1, NX)]
        self.z_peer = [device(x, lax.rem(z + d, NZ), y_hi, y_lo, core) for d in range(1, NZ)]
        self.y_peer = device(x, z, 1 - y_hi, y_lo, core)

    def copy(self, src, dst, send, recv, peer):
        return pltpu.make_async_remote_copy(
            src_ref=src, dst_ref=dst, send_sem=send, recv_sem=recv, device_id=peer, device_id_type=MESH
        )

    def x_reduce(self):
        return [
            self.copy(self.xs.at[lax.rem(self.x + d, NX)], self.xr.at[d - 1], self.sem3.at[0, d - 1], self.sem3.at[1, d - 1], self.x_peer[d - 1])
            for d in range(1, NX)
        ]

    def z_reduce(self):
        return [
            self.copy(self.zs.at[lax.rem(self.z + d, NZ)], self.zr.at[d - 1], self.sem7.at[0, d - 1], self.sem7.at[1, d - 1], self.z_peer[d - 1])
            for d in range(1, NZ)
        ]

    def y_swap(self):
        return self.copy(self.yf, self.yr, self.sem1.at[0], self.sem1.at[1], self.y_peer)

    def z_gather(self, sender):
        out = []
        for d in range(1, NZ):
            block = self.full.at[self.x, self.z if sender else lax.rem(self.z + NZ - d, NZ)]
            out.append(self.copy(block, block, self.sem7.at[2, d - 1], self.sem7.at[3, d - 1], self.z_peer[d - 1]))
        return out

    def x_gather(self, sender):
        out = []
        for d in range(1, NX):
            block = self.full.at[self.x if sender else lax.rem(self.x + NX - d, NX)]
            out.append(self.copy(block, block, self.sem3.at[2, d - 1], self.sem3.at[3, d - 1], self.x_peer[d - 1]))
        return out

    def step1(self):
        self.xs[...] = self.acc[...].astype(BF16)
        for c in self.x_reduce():
            c.start()

    def step2(self):
        for c in self.x_reduce():
            c.wait_recv()
        total = self.acc[self.x]
        for d in range(NX - 1):
            total = total + self.xr[d].astype(F32)
        for t in range(NZ):
            tile = total[:, t * W : (t + 1) * W]
            self.zf[t] = tile
            self.zs[t] = tile.astype(BF16)
        for c in self.z_reduce():
            c.start()

    def step3(self):
        for c in self.z_reduce():
            c.wait_recv()
        total = self.zf[self.z]
        for d in range(NZ - 1):
            total = total + self.zr[d].astype(F32)
        self.yf[...] = total
        self.y_swap().start()

    def step4(self):
        self.y_swap().wait_recv()
        self.full[self.x, self.z] = (self.yf[...] + self.yr[...]).astype(BF16)
        for c in self.z_gather(True):
            c.start()

    def step5(self):
        for c in self.z_gather(False):
            c.wait_recv()
        for c in self.x_gather(True):
            c.start()

    def step6(self):
        for c in self.x_gather(False):
            c.wait_recv()

    def drain(self):
        for c in self.x_reduce() + self.z_reduce() + [self.y_swap()] + self.z_gather(True) + self.x_gather(True):
            c.wait_send()

    def columns(self, first, tiles):
        strips = [jnp.concatenate([self.full[k, t] for k in range(NX)], axis=0) for t in range(first, first + tiles)]
        return jnp.concatenate(strips, axis=1)


def group_scratch(depth):
    return [
        pltpu.VMEM((NX, depth, WIDE), F32),
        pltpu.VMEM((NX, depth, WIDE), BF16),
        pltpu.VMEM((NX - 1, depth, WIDE), BF16),
        pltpu.VMEM((NZ, depth, W), F32),
        pltpu.VMEM((NZ, depth, W), BF16),
        pltpu.VMEM((NZ - 1, depth, W), BF16),
        pltpu.VMEM((depth, W), F32),
        pltpu.VMEM((depth, W), F32),
        pltpu.VMEM((NX, NZ, depth, W), BF16),
        pltpu.SemaphoreType.DMA((4, NX - 1)),
        pltpu.SemaphoreType.DMA((4, NZ - 1)),
        pltpu.SemaphoreType.DMA((2,)),
    ]


PER_GROUP = 12


def gather_and_reduce(e_hbm, p_hbm, t_hbm, e, g, y, t, *scratch):
    groups = [Group(depth, scratch[k * PER_GROUP : (k + 1) * PER_GROUP]) for k, depth in enumerate(GROUPS)]
    load_sem, core_sem, y_sem, fwd_sem = scratch[len(GROUPS) * PER_GROUP :]
    x, z, y_hi, y_lo, core = place()
    for group in groups:
        group.bind(x, z, y_hi, y_lo, core)
    own, other = 2 * y_lo, 2 * (1 - y_lo)
    sibling = device(x, z, y_hi, y_lo, 1 - core)
    partner = device(x, z, y_hi, 1 - y_lo, core)

    load_p = pltpu.make_async_copy(p_hbm, g.at[own + core], load_sem.at[0])
    load_e = pltpu.make_async_copy(e_hbm, e, load_sem.at[1])
    load_t = pltpu.make_async_copy(t_hbm, t, load_sem.at[2])
    load_p.start()
    load_e.start()
    load_t.start()

    barrier = pltpu.get_barrier_semaphore()
    peers = [sibling, partner, groups[0].y_peer] + groups[0].x_peer + groups[0].z_peer
    for peer in peers:
        pl.semaphore_signal(barrier, inc=1, device_id=peer, device_id_type=MESH)
    pl.semaphore_wait(barrier, len(peers))

    def remote(src, dst, send, recv, peer):
        return pltpu.make_async_remote_copy(
            src_ref=src, dst_ref=dst, send_sem=send, recv_sem=recv, device_id=peer, device_id_type=MESH
        )

    def share(part, owner):
        half = (1 - owner) if part == 0 else owner
        block = g.at[own + owner, pl.ds(pl.multiple_of(half * HALF, HALF), HALF)]
        return remote(block, block, core_sem.at[0, part], core_sem.at[1, part], sibling)

    def rows_of(half, k):
        return pl.ds(pl.multiple_of(half * HALF + k * CHUNK, CHUNK), CHUNK)

    def across(first, j, k):
        block = g.at[first + j, rows_of(core, k)]
        return remote(block, block, y_sem.at[0, j, k], y_sem.at[1, j, k], partner)

    def forward(half, j, k):
        block = g.at[other + j, rows_of(half, k)]
        return remote(block, block, fwd_sem.at[0, j, k], fwd_sem.at[1, j, k], sibling)

    load_p.wait()
    share(0, core).start()

    @pl.when(core == 0)
    def _():
        for k in range(CHUNKS):
            across(own, 0, k).start()

    share(1, core).start()
    share(0, 1 - core).wait_recv()

    @pl.when(core == 1)
    def _():
        for k in range(CHUNKS):
            across(own, 0, k).start()

    for k in range(CHUNKS):
        across(own, 1, k).start()

    share(1, 1 - core).wait_recv()
    load_e.wait()

    def wide(rows, tile):
        if tile < 3:
            return e[rows, tile * 256 : (tile + 1) * 256]
        return jnp.concatenate([g[own, rows], g[own + 1, rows]], axis=1)

    def project(group, blocks, rows, start):
        left = jnp.concatenate([g[b, rows] for b in blocks], axis=1) if len(blocks) > 1 else g[blocks[0], rows]
        for tile in range(4):
            part = tdot(left, wide(rows, tile)).reshape(NX, group.depth, 256)
            where = (slice(None), slice(None), slice(tile * 256, (tile + 1) * 256))
            if start:
                group.acc[where] = part
            else:
                group.acc[where] += part

    first, middle, last = groups
    project(first, [own, own + 1], pl.ds(0, CHUNK), True)

    @pl.loop(1, ROWS // CHUNK)
    def _(k):
        project(first, [own, own + 1], pl.ds(pl.multiple_of(k * CHUNK, CHUNK), CHUNK), False)

    first.step1()

    def arrive(j, k, group):
        across(other, j, k).wait_recv()
        forward(core, j, k).start()
        project(group, [other + j], rows_of(core, k), k == 0)
        forward(1 - core, j, k).wait_recv()
        project(group, [other + j], rows_of(1 - core, k), False)

    arrive(0, 0, middle)
    arrive(0, 1, middle)
    first.step2()
    arrive(0, 2, middle)
    middle.step1()
    arrive(1, 0, last)
    first.step3()
    arrive(1, 1, last)
    first.step4()
    middle.step2()
    arrive(1, 2, last)
    last.step1()
    middle.step3()
    first.step5()
    middle.step4()
    last.step2()
    middle.step5()
    last.step3()
    last.step4()
    last.step5()
    load_t.wait()
    t0_high, t0_low = split(t[0])
    t1_high, t1_low = split(t[1])
    first.step6()
    middle.step6()
    last.step6()

    def finish(p1, p2, cross, transposed):
        for n in range(3):
            lead_in = p1(n)
            lead = (dot(t0_high, lead_in) + dot(t0_low, lead_in)).astype(BF16)
            y[0:256, n * 256 : (n + 1) * 256] = lead
            pulled = tdot(cross, lead) if transposed else dot(cross, lead)
            high, low = split(p2(n).astype(F32) - pulled)
            trail = dot(t1_high, high) + dot(t1_high, low) + dot(t1_low, high)
            y[256:512, n * 256 : (n + 1) * 256] = trail.astype(BF16)

    def mine(n):
        return first.columns(2 * n, 2)

    def theirs(n):
        return jnp.concatenate([middle.columns(2 * n, 2), last.columns(2 * n, 2)], axis=0)

    @pl.when(y_lo == 0)
    def _():
        finish(mine, theirs, theirs(3), False)

    @pl.when(y_lo == 1)
    def _():
        finish(theirs, mine, theirs(3), True)

    share(0, core).wait_send()
    share(1, core).wait_send()
    for j in range(2):
        for k in range(CHUNKS):
            across(own, j, k).wait_send()
            forward(core, j, k).wait_send()
    for group in groups:
        group.drain()


BLOCK = 512


def update(e, g, y, out):
    rows = pl.ds(pl.multiple_of(pl.program_id(0) * BLOCK, BLOCK), BLOCK)
    left = jnp.concatenate([g[b, rows] for b in range(4)], axis=1)
    for n in range(3):
        where = slice(n * 256, (n + 1) * 256)
        out[:, where] = (e[rows, where].astype(F32) - dot(left, y[:, where])).astype(BF16)


def per_device(eigvecs, panels, t_factors):
    scratch = [pltpu.VMEM((2, 256, 256), F32)]
    for depth in GROUPS:
        scratch += group_scratch(depth)
    scratch += [
        pltpu.SemaphoreType.DMA((3,)),
        pltpu.SemaphoreType.DMA((2, 2)),
        pltpu.SemaphoreType.DMA((2, 2, CHUNKS)),
        pltpu.SemaphoreType.DMA((2, 2, CHUNKS)),
    ]
    hbm = pl.BlockSpec(memory_space=pltpu.HBM)
    vmem = pl.BlockSpec(memory_space=pltpu.VMEM)
    e, g, y = pl.pallas_call(
        gather_and_reduce,
        out_shape=(
            pltpu.VMEM((ROWS, COLS), BF16),
            pltpu.VMEM((4, ROWS, W), BF16),
            pltpu.VMEM((512, COLS), BF16),
        ),
        in_specs=[hbm] * 3,
        out_specs=(vmem,) * 3,
        scratch_shapes=scratch,
        compiler_params=pltpu.CompilerParams(collective_id=0, has_side_effects=True, vmem_limit_bytes=32 << 20),
        name="gather_and_reduce",
    )(*[pltpu.with_memory_space_constraint(a, pltpu.HBM) for a in (eigvecs, panels, t_factors)])
    return pl.pallas_call(
        update,
        out_shape=jax.ShapeDtypeStruct((ROWS, COLS), BF16),
        grid=(ROWS // BLOCK,),
        in_specs=[vmem] * 3,
        out_specs=pl.BlockSpec((BLOCK, COLS), lambda i: (i, 0)),
        compiler_params=pltpu.CompilerParams(vmem_limit_bytes=24 << 20),
        name="update",
    )(e, g, y)


def solution(mesh):
    in_specs = (P("row", "col"), P("row", "col"), P())
    return jax.shard_map(per_device, mesh=mesh, in_specs=in_specs, out_specs=P("row", "col"), check_vma=False)
```

time: 1410 us -> 69.2 us (0.05); the launches traced: 1390 us -> 69.1 us
  waiting for transfers between devices: 1340 us -> 0 us
  Pallas kernels: 0 us -> 69.1 us
  matrix products: 20.8 us -> 0 us
  local copies, waits for them, and re-layouts: 14.2 us -> 0 us
    psum x2 -> x0, waiting for transfers between devices: 1300 us -> none  [finish(): summed = lax.psum(partial_value, 'row')]
    pallas_call x0 -> x2, Pallas kernels: none -> 69.1 us  [the longest x1 64.1 us: per_device(): pl.pallas_call(gather_and_reduce, out_shape=(pltpu.VMEM((ROWS, COLS), BF1...]
    all_gather x1 -> x0, waiting for transfers between devices: 43.9 us -> none  [per_device(): gathered = lax.all_gather(panels, 'col', axis=1, tiled=True)]
    dot_general x6 -> x0, matrix products: 20.8 us -> none  [the longest x1 7 us: per_device(): update = jnp.dot(gathered, stacked, preferred_element_type=jnp.float32)]
  transfers between devices with their start and end apart: 3 -> 0, of which waited for: 3 -> 0; matrix products, arithmetic and copies ran while one was open for 1% -> 0% of each run, Pallas kernels for 0% -> 0%
where the time goes in v1:
time: 69.2 us; the launch traced here: 69.1 us
  Pallas kernels  69.1 us (100%)
    pallas_call x1, Pallas kernels, per_device(): pl.pallas_call(gather_and_reduce, out_shape=(pltpu.VMEM((ROWS, COLS), BF1...  64.1 us
    pallas_call x1, Pallas kernels, per_device(): pl.pallas_call(update, out_shape=jax.ShapeDtypeStruct((ROWS, COLS), BF16)...  4.98 us

profile of v1, /device:TPU:4, one launch (start us, length us, event | category | flops | bytes accessed | tf_op | source)
XLA Modules:
  0.0 69.1 jit_solution(12744927032736046635)
XLA Ops:
  0.0 64.1 %gather_and_reduce.1 = (bf16[3072,768]{1,0:T(8,128)(2,1)S(1)}, bf16[4,3072,128]{2,1,0:T(8,128)(2,1)S(1)}, bf16[512,768]{1,0:T(8,128)(2,1)S(1)}) custom-call(bf16[3072,768]{1,0:T(8,128)(2,1)} %e_hbm.1, bf16[3072,128]{1,0:T(8,128)(2,1)} %p_hbm.1, f32[2,256,256]{2,1,0:T(8,128)} %t_hbm.1), custom_call_target="tpu_custom_call" | custom-call | tf_op jit(solution)/shard_map/gather_and_reduce/pallas_call | solution.py:344
  64.1 5.0 %update.1 = bf16[3072,768]{1,0:T(8,128)(2,1)} custom-call(bf16[3072,768]{1,0:T(8,128)(2,1)S(1)} %get-tuple-element.8.e, bf16[4,3072,128]{2,1,0:T(8,128)(2,1)S(1)} %get-tuple-element.9.g, bf16[512,768]{1,0:T(8,128)(2,1)S(1)} %get-tuple-element.10.y), custom_call_target="tpu_custom_call" | custom-call | tf_op jit(solution)/shard_map/update/pallas_call | solution.py:357

commit v2 on v1

--- a/solution.py
+++ b/solution.py
@@ -1,5 +1,3 @@
-import functools
-
 import jax
 import jax.numpy as jnp
 from jax import lax
@@ -16,7 +14,8 @@
 HALF = ROWS // 2
 CHUNKS = 3
 CHUNK = HALF // CHUNKS
-GROUPS = (64, 32, 32)
+DEPTH = 2
+GROUPS = ((64, 6), (32, 8), (32, 8))
 BF16 = jnp.bfloat16
 F32 = jnp.float32
 
@@ -44,8 +43,8 @@
 
 
 class Group:
-    def __init__(self, depth, refs):
-        self.depth = depth
+    def __init__(self, depth, tiles, refs):
+        self.depth, self.tiles, self.part = depth, tiles, depth * tiles // NZ
         (self.acc, self.xs, self.xr, self.zf, self.zs, self.zr, self.yf, self.yr, self.full, self.sem3, self.sem7, self.sem1) = refs
 
     def bind(self, x, z, y_hi, y_lo, core):
@@ -59,6 +58,9 @@
             src_ref=src, dst_ref=dst, send_sem=send, recv_sem=recv, device_id=peer, device_id_type=MESH
         )
 
+    def slot(self, z):
+        return pl.ds(pl.multiple_of(z * self.part, 16), self.part)
+
     def x_reduce(self):
         return [
             self.copy(self.xs.at[lax.rem(self.x + d, NX)], self.xr.at[d - 1], self.sem3.at[0, d - 1], self.sem3.at[1, d - 1], self.x_peer[d - 1])
@@ -67,7 +69,7 @@
 
     def z_reduce(self):
         return [
-            self.copy(self.zs.at[lax.rem(self.z + d, NZ)], self.zr.at[d - 1], self.sem7.at[0, d - 1], self.sem7.at[1, d - 1], self.z_peer[d - 1])
+            self.copy(self.zs.at[self.slot(lax.rem(self.z + d, NZ))], self.zr.at[d - 1], self.sem7.at[0, d - 1], self.sem7.at[1, d - 1], self.z_peer[d - 1])
             for d in range(1, NZ)
         ]
 
@@ -77,7 +79,7 @@
     def z_gather(self, sender):
         out = []
         for d in range(1, NZ):
-            block = self.full.at[self.x, self.z if sender else lax.rem(self.z + NZ - d, NZ)]
+            block = self.full.at[self.x, self.slot(self.z if sender else lax.rem(self.z + NZ - d, NZ))]
             out.append(self.copy(block, block, self.sem7.at[2, d - 1], self.sem7.at[3, d - 1], self.z_peer[d - 1]))
         return out
 
@@ -99,17 +101,17 @@
         total = self.acc[self.x]
         for d in range(NX - 1):
             total = total + self.xr[d].astype(F32)
-        for t in range(NZ):
-            tile = total[:, t * W : (t + 1) * W]
-            self.zf[t] = tile
-            self.zs[t] = tile.astype(BF16)
+        for t in range(self.tiles):
+            tile, where = total[:, t * W : (t + 1) * W], slice(t * self.depth, (t + 1) * self.depth)
+            self.zf[where] = tile
+            self.zs[where] = tile.astype(BF16)
         for c in self.z_reduce():
             c.start()
 
     def step3(self):
         for c in self.z_reduce():
             c.wait_recv()
-        total = self.zf[self.z]
+        total = self.zf[self.slot(self.z)]
         for d in range(NZ - 1):
             total = total + self.zr[d].astype(F32)
         self.yf[...] = total
@@ -117,15 +119,22 @@
 
     def step4(self):
         self.y_swap().wait_recv()
-        self.full[self.x, self.z] = (self.yf[...] + self.yr[...]).astype(BF16)
+        self.full[self.x, self.slot(self.z)] = (self.yf[...] + self.yr[...]).astype(BF16)
         for c in self.z_gather(True):
             c.start()
 
-    def step5(self):
+    def step5(self, which=None):
         for c in self.z_gather(False):
             c.wait_recv()
-        for c in self.x_gather(True):
-            c.start()
+        if which is None: which=range(NX-1)
+        cs = self.x_gather(True)
+        for d in which:
+            cs[d].start()
+
+    def step5b(self, which):
+        cs = self.x_gather(True)
+        for d in which:
+            cs[d].start()
 
     def step6(self):
         for c in self.x_gather(False):
@@ -136,21 +145,23 @@
             c.wait_send()
 
     def columns(self, first, tiles):
-        strips = [jnp.concatenate([self.full[k, t] for k in range(NX)], axis=0) for t in range(first, first + tiles)]
+        n = self.depth
+        strips = [jnp.concatenate([self.full[k, t * n : (t + 1) * n] for k in range(NX)], axis=0) for t in range(first, first + tiles)]
         return jnp.concatenate(strips, axis=1)
 
 
-def group_scratch(depth):
+def group_scratch(depth, tiles):
+    wide, flat, part = tiles * W, tiles * depth, tiles * depth // NZ
     return [
-        pltpu.VMEM((NX, depth, WIDE), F32),
-        pltpu.VMEM((NX, depth, WIDE), BF16),
-        pltpu.VMEM((NX - 1, depth, WIDE), BF16),
-        pltpu.VMEM((NZ, depth, W), F32),
-        pltpu.VMEM((NZ, depth, W), BF16),
-        pltpu.VMEM((NZ - 1, depth, W), BF16),
-        pltpu.VMEM((depth, W), F32),
-        pltpu.VMEM((depth, W), F32),
-        pltpu.VMEM((NX, NZ, depth, W), BF16),
+        pltpu.VMEM((NX, depth, wide), F32),
+        pltpu.VMEM((NX, depth, wide), BF16),
+        pltpu.VMEM((NX - 1, depth, wide), BF16),
+        pltpu.VMEM((flat, W), F32),
+        pltpu.VMEM((flat, W), BF16),
+        pltpu.VMEM((NZ - 1, part, W), BF16),
+        pltpu.VMEM((part, W), F32),
+        pltpu.VMEM((part, W), F32),
+        pltpu.VMEM((NX, flat, W), BF16),
         pltpu.SemaphoreType.DMA((4, NX - 1)),
         pltpu.SemaphoreType.DMA((4, NZ - 1)),
         pltpu.SemaphoreType.DMA((2,)),
@@ -161,7 +172,7 @@
 
 
 def gather_and_reduce(e_hbm, p_hbm, t_hbm, e, g, y, t, *scratch):
-    groups = [Group(depth, scratch[k * PER_GROUP : (k + 1) * PER_GROUP]) for k, depth in enumerate(GROUPS)]
+    groups = [Group(*size, scratch[k * PER_GROUP : (k + 1) * PER_GROUP]) for k, size in enumerate(GROUPS)]
     load_sem, core_sem, y_sem, fwd_sem = scratch[len(GROUPS) * PER_GROUP :]
     x, z, y_hi, y_lo, core = place()
     for group in groups:
@@ -206,22 +217,23 @@
 
     load_p.wait()
     share(0, core).start()
+    order = [(j, k) for j in range(2) for k in range(CHUNKS)]
 
     @pl.when(core == 0)
     def _():
-        for k in range(CHUNKS):
-            across(own, 0, k).start()
+        for j, k in order[:min(DEPTH,CHUNKS)]:
+            across(own, j, k).start()
 
     share(1, core).start()
     share(0, 1 - core).wait_recv()
 
     @pl.when(core == 1)
     def _():
-        for k in range(CHUNKS):
-            across(own, 0, k).start()
-
-    for k in range(CHUNKS):
-        across(own, 1, k).start()
+        for j, k in order[:min(DEPTH,CHUNKS)]:
+            across(own, j, k).start()
+
+    for j, k in order[min(DEPTH,CHUNKS):DEPTH]:
+        across(own, j, k).start()
 
     share(1, 1 - core).wait_recv()
     load_e.wait()
@@ -233,7 +245,7 @@
 
     def project(group, blocks, rows, start):
         left = jnp.concatenate([g[b, rows] for b in blocks], axis=1) if len(blocks) > 1 else g[blocks[0], rows]
-        for tile in range(4):
+        for tile in range(group.tiles // 2):
             part = tdot(left, wide(rows, tile)).reshape(NX, group.depth, 256)
             where = (slice(None), slice(None), slice(tile * 256, (tile + 1) * 256))
             if start:
@@ -252,30 +264,29 @@
 
     def arrive(j, k, group):
         across(other, j, k).wait_recv()
+        n = j * CHUNKS + k + DEPTH
+        if n < len(order): across(own, *order[n]).start()
         forward(core, j, k).start()
         project(group, [other + j], rows_of(core, k), k == 0)
         forward(1 - core, j, k).wait_recv()
         project(group, [other + j], rows_of(1 - core, k), False)
 
-    arrive(0, 0, middle)
-    arrive(0, 1, middle)
-    first.step2()
-    arrive(0, 2, middle)
-    middle.step1()
-    arrive(1, 0, last)
-    first.step3()
-    arrive(1, 1, last)
-    first.step4()
-    middle.step2()
-    arrive(1, 2, last)
+    C = CHUNKS
+    hooks = {(0, C - 2 if C > 2 else C - 1): [first.step2], (0, C - 1): [middle.step1], (1, max(0, C - 3)): [first.step3], (1, C - 2): [first.step4, middle.step2]}
+    for j in range(2):
+        for k in range(C):
+            arrive(j, k, (middle, last)[j])
+            for h in hooks.get((j, k), []):
+                h()
     last.step1()
+    last.step2()
     middle.step3()
-    first.step5()
+    first.step5([0, 2])
+    last.step3()
     middle.step4()
-    last.step2()
+    first.step5b([1])
+    last.step4()
     middle.step5()
-    last.step3()
-    last.step4()
     last.step5()
     load_t.wait()
     t0_high, t0_low = split(t[0])
@@ -318,7 +329,7 @@
         group.drain()
 
 
-BLOCK = 512
+BLOCK = 1024
 
 
 def update(e, g, y, out):
@@ -331,8 +342,8 @@
 
 def per_device(eigvecs, panels, t_factors):
     scratch = [pltpu.VMEM((2, 256, 256), F32)]
-    for depth in GROUPS:
-        scratch += group_scratch(depth)
+    for size in GROUPS:
+        scratch += group_scratch(*size)
     scratch += [
         pltpu.SemaphoreType.DMA((3,)),
         pltpu.SemaphoreType.DMA((2, 2)),

time: 69.2 us -> 60.5 us (0.87)
  Pallas kernels: 69.1 us -> 60.2 us
    pallas_call x1, Pallas kernels: 64.1 us -> 56 us  [per_device(): pl.pallas_call(gather_and_reduce, out_shape=(pltpu.VMEM((ROWS, COLS), BF1...]
    pallas_call x1, Pallas kernels: 4.98 us -> 4.27 us  [per_device(): pl.pallas_call(update, out_shape=jax.ShapeDtypeStruct((ROWS, COLS), BF16)...]
where the time goes in v2:
time: 60.5 us; the launch traced here: 60.3 us
  Pallas kernels  60.2 us (100%)
    pallas_call x1, Pallas kernels, per_device(): pl.pallas_call(gather_and_reduce, out_shape=(pltpu.VMEM((ROWS, COLS), BF1...  56 us
    pallas_call x1, Pallas kernels, per_device(): pl.pallas_call(update, out_shape=jax.ShapeDtypeStruct((ROWS, COLS), BF16)...  4.27 us

profile of v2, /device:TPU:4, one launch (start us, length us, event | category | flops | bytes accessed | tf_op | source)
XLA Modules:
  0.0 60.3 jit_solution(4302775839556380928)
XLA Ops:
  0.0 56.0 %gather_and_reduce.1 = (bf16[3072,768]{1,0:T(8,128)(2,1)S(1)}, bf16[4,3072,128]{2,1,0:T(8,128)(2,1)S(1)}, bf16[512,768]{1,0:T(8,128)(2,1)S(1)}) custom-call(bf16[3072,768]{1,0:T(8,128)(2,1)} %e_hbm.1, bf16[3072,128]{1,0:T(8,128)(2,1)} %p_hbm.1, f32[2,256,256]{2,1,0:T(8,128)} %t_hbm.1), custom_call_target="tpu_custom_call" | custom-call | tf_op jit(solution)/shard_map/gather_and_reduce/pallas_call | solution.py:355
  56.0 4.3 %update.1 = bf16[3072,768]{1,0:T(8,128)(2,1)} custom-call(bf16[3072,768]{1,0:T(8,128)(2,1)S(1)} %get-tuple-element.8.e, bf16[4,3072,128]{2,1,0:T(8,128)(2,1)S(1)} %get-tuple-element.9.g, bf16[512,768]{1,0:T(8,128)(2,1)S(1)} %get-tuple-element.10.y), custom_call_target="tpu_custom_call" | custom-call | tf_op jit(solution)/shard_map/update/pallas_call | solution.py:368

commit v3 on v2

--- a/solution.py
+++ b/solution.py
@@ -14,7 +14,7 @@
 HALF = ROWS // 2
 CHUNKS = 3
 CHUNK = HALF // CHUNKS
-DEPTH = 2
+DEPTH = 3
 GROUPS = ((64, 6), (32, 8), (32, 8))
 BF16 = jnp.bfloat16
 F32 = jnp.float32
@@ -281,13 +281,13 @@
     last.step1()
     last.step2()
     middle.step3()
-    first.step5([0, 2])
+    first.step5([1])
     last.step3()
     middle.step4()
-    first.step5b([1])
+    first.step5b([0,2])
     last.step4()
-    middle.step5()
-    last.step5()
+    middle.step5([1, 0, 2])
+    last.step5([1, 0, 2])
     load_t.wait()
     t0_high, t0_low = split(t[0])
     t1_high, t1_low = split(t[1])
@@ -329,7 +329,7 @@
         group.drain()
 
 
-BLOCK = 1024
+BLOCK = 1536
 
 
 def update(e, g, y, out):

time: 60.5 us -> 60.5 us (level); the launches traced: 60.3 us -> 59.4 us
  Pallas kernels: 60.2 us -> 59.4 us
    pallas_call x1, Pallas kernels: 56 us -> 55.2 us  [per_device(): pl.pallas_call(gather_and_reduce, out_shape=(pltpu.VMEM((ROWS, COLS), BF1...]
where the time goes in v3:
time: 60.5 us; the launch traced here: 59.4 us
  Pallas kernels  59.4 us (98%)
    pallas_call x1, Pallas kernels, per_device(): pl.pallas_call(gather_and_reduce, out_shape=(pltpu.VMEM((ROWS, COLS), BF1...  55.2 us
    pallas_call x1, Pallas kernels, per_device(): pl.pallas_call(update, out_shape=jax.ShapeDtypeStruct((ROWS, COLS), BF16)...  4.23 us

profile of v3, /device:TPU:4, one launch (start us, length us, event | category | flops | bytes accessed | tf_op | source)
XLA Modules:
  0.0 59.4 jit_solution(14348493610040476365)
XLA Ops:
  0.0 55.2 %gather_and_reduce.1 = (bf16[3072,768]{1,0:T(8,128)(2,1)S(1)}, bf16[4,3072,128]{2,1,0:T(8,128)(2,1)S(1)}, bf16[512,768]{1,0:T(8,128)(2,1)S(1)}) custom-call(bf16[3072,768]{1,0:T(8,128)(2,1)} %e_hbm.1, bf16[3072,128]{1,0:T(8,128)(2,1)} %p_hbm.1, f32[2,256,256]{2,1,0:T(8,128)} %t_hbm.1), custom_call_target="tpu_custom_call" | custom-call | tf_op jit(solution)/shard_map/gather_and_reduce/pallas_call | solution.py:355
  55.2 4.2 %update.1 = bf16[3072,768]{1,0:T(8,128)(2,1)} custom-call(bf16[3072,768]{1,0:T(8,128)(2,1)S(1)} %get-tuple-element.8.e, bf16[4,3072,128]{2,1,0:T(8,128)(2,1)S(1)} %get-tuple-element.9.g, bf16[512,768]{1,0:T(8,128)(2,1)S(1)} %get-tuple-element.10.y), custom_call_target="tpu_custom_call" | custom-call | tf_op jit(solution)/shard_map/update/pallas_call | solution.py:368
